TPU v7x, 32 devices: a whole 2x2x4 slice. The times are simulated.
32 devices in a mesh: ctx: 8 (over z, x), head: 2 (over core), exp: 2 (over y).
Axes of the slice: x: 2, y: 2, z: 4, core: 2. Of those that a mesh axis runs over, the one named last changes fastest.
Arguments:
- residual: bfloat16 [1024, 4096], P(('ctx', 'exp')), may hold values from -40 to 40
- queries: bfloat16 [1024, 8192], P('ctx', ('head', 'exp')), may hold values from -5 to 5
- key_head_array: bfloat16 [1024, 512], P('ctx', 'head'), may hold values from -5 to 5
- value_head_array: bfloat16 [1024, 512], P('ctx', 'head'), may hold values from -6 to 6
- doc_ids: int32 [1024], P('ctx'), may hold values from 0 to 7, never falling along the last dimension, each value on 1 to 384 neighbouring positions
- out_weight: bfloat16 [8192, 4096], P(('head', 'exp'), 'ctx'), may hold values from -0.0625 to 0.0625
- norm_gain: float32 [4096], replicated, may hold values from 0.1 to 1.9
- routes: int32 [1024, 8], P(('ctx', 'exp')), may hold values from 0 to 15, all different within a row; in each aligned block of 64 rows (0 to 63, 64 to 127, ...) at most 48 rows name the same one
- gate_probs: float32 [1024, 8], P(('ctx', 'exp')), may hold values from 0.05 to 0.5
- expert_gate: bfloat16 [16, 4096, 768], P(('ctx', 'exp'), None, 'head'), may hold values from -0.09375 to 0.09375
- expert_up: bfloat16 [16, 4096, 768], P(('ctx', 'exp'), None, 'head'), may hold values from -0.09375 to 0.09375
- expert_down: bfloat16 [16, 768, 4096], P(('ctx', 'exp'), 'head'), may hold values from -0.21875 to 0.21875
- grad_out: bfloat16 [1024, 4096], P(('ctx', 'exp')), may hold values from -6 to 6
Outputs:
- layer_out: bfloat16 [1024, 4096], P(('ctx', 'exp'))
- grad_resid: bfloat16 [1024, 4096], P(('ctx', 'exp'))
- grad_queries: bfloat16 [1024, 8192], P('ctx', ('head', 'exp'))
- grad_keys: bfloat16 [1024, 512], P(('ctx', 'exp'), 'head')
- grad_values: bfloat16 [1024, 512], P(('ctx', 'exp'), 'head')
Inputs may be any that keep to these rules, and one draw needn't show every extreme that they name: `routes`: each row names 8 different experts; within each aligned block of 64 rows (the rows of one device) no expert is named by more than 48 rows, a bound that some block reaches. `doc_ids`: never falls along the sequence; each document has 1 to 384 tokens and one has exactly 384.
All inputs are finite; a program needn't handle non-finite values.
Results may differ from a plain program's by a relative error of at most 0.024.
Values may be sent and summed in bfloat16 or wider, within the bound.
No kernel may reach another device: no remote copies, remote signals or barrier semaphores. Data moves between devices by JAX's collectives and lax.ppermute only.
A program may use at most 192 MiB of HBM per device.

v0:
```python
import math

import jax
import jax.numpy as jnp
from jax import lax
from jax.sharding import PartitionSpec as P

HEAD_SIZE = 128
QUERY_HEADS = 64
KEY_VALUE_HEADS = 4
SPAN = 4


neg_large = -1e30
eps_norm = 1e-06


def from_behind(value, axis, steps):
    count = lax.axis_size(axis)
    leading, last = (max(0, -steps), min(count, count - steps))
    return lax.ppermute(value, axis, [(source, source + steps) for source in range(leading, last)])


def as_sent(value):
    return jax.tree.map(lambda a: a.astype(jnp.bfloat16) if a.dtype == jnp.float32 else a, value)


def rms_normed(hidden, norm_gain):
    factor = lax.rsqrt(jnp.mean(hidden * hidden, axis=-1, keepdims=True) + eps_norm)
    return hidden * factor * norm_gain


def block_mask(query_docs, key_docs, query_base, key_base):
    query_pos = query_base + jnp.arange(query_docs.shape[0], dtype=jnp.int32)
    key_pos = key_base + jnp.arange(key_docs.shape[0], dtype=jnp.int32)
    same_doc = query_docs[:, None] == key_docs[None, :]
    return same_doc & (key_pos[None, :] <= query_pos[:, None]) & (key_base >= 0)


def local(
    residual,
    queries,
    key_head_array,
    value_head_array,
    doc_ids,
    out_weight,
    norm_gain,
    routes,
    gate_probs,
    expert_gate,
    expert_up,
    expert_down,
    grad_out,
):
    tokens = queries.shape[0]
    head_count = queries.shape[1] // HEAD_SIZE
    score_scale = 1.0 / math.sqrt(HEAD_SIZE)
    group_width = QUERY_HEADS // KEY_VALUE_HEADS
    ctx_index = lax.axis_index("ctx")
    pair_index = lax.axis_index("exp") * head_count // group_width
    own_keys = lax.dynamic_slice_in_dim(key_head_array, pair_index * HEAD_SIZE, HEAD_SIZE, 1)
    own_values = lax.dynamic_slice_in_dim(value_head_array, pair_index * HEAD_SIZE, HEAD_SIZE, 1)
    query_heads = queries.reshape(tokens, head_count, HEAD_SIZE)
    query_base = ctx_index * tokens
    blocks = [(own_keys, own_values, doc_ids)]
    for distance in range(1, SPAN):
        blocks.append(tuple(from_behind((blocks[-1][0], blocks[-1][1], blocks[-1][2]), "ctx", 1)))
    visible_masks = [
        block_mask(doc_ids, blocks[distance][2], query_base, (ctx_index - distance) * tokens)
        for distance in range(SPAN)
    ]
    carried = (
        jnp.full((tokens, head_count), neg_large, jnp.float32),
        jnp.zeros((tokens, head_count), jnp.float32),
        jnp.zeros((tokens, head_count, HEAD_SIZE), jnp.float32),
    )
    for distance in range(SPAN):
        key_block, value_block, docs_block = blocks[distance]
        attend_running, attend_row_total, attend_weighted = carried
        attend_scores = (
            jnp.einsum("qhd,kd->qhk", query_heads, key_block, preferred_element_type=jnp.float32)
            * score_scale
        )
        attend_scores = jnp.where(visible_masks[distance][:, None, :], attend_scores, neg_large)
        updated = jnp.maximum(attend_running, jnp.max(attend_scores, axis=-1))
        shrink = jnp.exp(attend_running - updated)
        weights = jnp.exp(attend_scores - updated[..., None])
        attend_row_total = attend_row_total * shrink + jnp.sum(weights, axis=-1)
        attend_weighted = attend_weighted * shrink[..., None] + jnp.einsum(
            "qhk,kd->qhd",
            weights.astype(jnp.bfloat16),
            value_block,
            preferred_element_type=jnp.float32,
        )
        carried = (updated, attend_row_total, attend_weighted)
    running, row_total, weighted = carried
    attn = (
        (weighted / row_total[..., None])
        .astype(jnp.bfloat16)
        .reshape(tokens, head_count * HEAD_SIZE)
    )
    log_total = running + jnp.log(row_total)
    out_full = lax.all_gather(out_weight, "ctx", axis=1, tiled=True)
    row_count = residual.shape[0]
    head_share = lax.psum_scatter(
        jnp.dot(attn, out_full, preferred_element_type=jnp.float32).astype(jnp.bfloat16),
        "exp",
        scatter_dimension=0,
        tiled=True,
    )
    attn_proj = lax.psum(head_share, "head").astype(jnp.float32)
    hidden = residual.astype(jnp.float32) + attn_proj
    normed_full, pullback = jax.vjp(lambda values: rms_normed(values, norm_gain), hidden)
    normed = normed_full.astype(jnp.bfloat16)
    ctx_size = lax.axis_size("ctx")
    exp_size = lax.axis_size("exp")
    expert_count = ctx_size * exp_size
    top_count = routes.shape[1]
    capacity = max(2, 3 * row_count * top_count // (2 * expert_count))
    model_width = normed.shape[1]
    flat_routes = routes.reshape(-1)
    onehot = (flat_routes[:, None] == jnp.arange(expert_count, dtype=jnp.int32)[None, :]).astype(
        jnp.int32
    )
    ranks = jnp.cumsum(onehot, axis=0) - 1
    slots = jnp.sum(ranks * onehot, axis=1)
    source_rows = jnp.arange(row_count * top_count, dtype=jnp.int32) // top_count
    send_normed = (
        jnp.zeros((expert_count, capacity, model_width), jnp.bfloat16)
        .at[flat_routes, slots]
        .set(normed[source_rows])
    )
    send_grads = (
        jnp.zeros((expert_count, capacity, model_width), jnp.bfloat16)
        .at[flat_routes, slots]
        .set(grad_out[source_rows])
    )
    gate_mat = expert_gate[0]
    up_mat = expert_up[0]
    down_mat = expert_down[0]
    contract = (((1,), (1,)), ((), ()))
    received_normed = lax.all_to_all(
        send_normed, ("ctx", "exp"), split_axis=0, concat_axis=0, tiled=True
    )
    shape_in = received_normed.shape
    rows_in = received_normed.reshape(-1, shape_in[-1])
    rows_grad = lax.all_to_all(
        send_grads, ("ctx", "exp"), split_axis=0, concat_axis=0, tiled=True
    ).reshape(-1, shape_in[-1])
    gate_pre = jnp.dot(rows_in, gate_mat, preferred_element_type=jnp.float32)
    up_pre = jnp.dot(rows_in, up_mat, preferred_element_type=jnp.float32)
    sigma = jax.nn.sigmoid(gate_pre)
    silu_val = gate_pre * sigma
    act = (silu_val * up_pre).astype(jnp.bfloat16)
    expert_out = jnp.dot(act, down_mat, preferred_element_type=jnp.float32).astype(jnp.bfloat16)
    back_act = lax.dot_general(rows_grad, down_mat, contract, preferred_element_type=jnp.float32)
    slope = sigma * (1.0 + gate_pre * (1.0 - sigma))
    grad_gate = (back_act * up_pre * slope).astype(jnp.bfloat16)
    grad_up = (back_act * silu_val).astype(jnp.bfloat16)
    grad_in = lax.dot_general(grad_gate, gate_mat, contract, preferred_element_type=jnp.float32)
    grad_in = (
        grad_in + lax.dot_general(grad_up, up_mat, contract, preferred_element_type=jnp.float32)
    ).astype(jnp.bfloat16)
    back_out = lax.all_to_all(
        expert_out.reshape(shape_in), ("ctx", "exp"), split_axis=0, concat_axis=0, tiled=True
    )
    back_grad = lax.all_to_all(
        grad_in.reshape(shape_in), ("ctx", "exp"), split_axis=0, concat_axis=0, tiled=True
    )
    picked_out = back_out[flat_routes, slots].reshape(row_count, top_count, model_width)
    picked_grad = back_grad[flat_routes, slots].reshape(row_count, top_count, model_width)
    moe_share = jnp.einsum("rk,rkd->rd", gate_probs, picked_out.astype(jnp.float32))
    norm_share = jnp.einsum("rk,rkd->rd", gate_probs, picked_grad.astype(jnp.float32))
    moe_sum, norm_grad = (
        lax.psum(moe_share.astype(jnp.bfloat16), "head").astype(jnp.float32),
        lax.psum(norm_share.astype(jnp.bfloat16), "head").astype(jnp.float32),
    )
    layer_out = (hidden + moe_sum).astype(jnp.bfloat16)
    grad_hidden = grad_out.astype(jnp.float32) + pullback(norm_grad)[0]
    grad_resid = grad_hidden.astype(jnp.bfloat16)
    grad_attn = lax.dot_general(
        lax.all_gather(grad_resid, "exp", axis=0, tiled=True),
        out_full,
        contract,
        preferred_element_type=jnp.float32,
    ).astype(jnp.bfloat16)
    grad_heads = grad_attn.reshape(tokens, head_count, HEAD_SIZE)
    attn_heads = attn.reshape(tokens, head_count, HEAD_SIZE)
    delta = jnp.sum(grad_heads.astype(jnp.float32) * attn_heads.astype(jnp.float32), axis=-1)
    grad_query_sum = jnp.zeros((tokens, head_count, HEAD_SIZE), jnp.float32)
    key_parts = []
    value_parts = []
    for distance in range(SPAN):
        key_block, value_block, docs_block = blocks[distance]
        scores = (
            jnp.einsum("qhd,kd->qhk", query_heads, key_block, preferred_element_type=jnp.float32)
            * score_scale
        )
        scores = jnp.where(visible_masks[distance][:, None, :], scores, neg_large)
        chances = jnp.exp(scores - log_total[..., None])
        grad_weights = jnp.einsum(
            "qhd,kd->qhk", grad_heads, value_block, preferred_element_type=jnp.float32
        )
        grad_scores = (chances * (grad_weights - delta[..., None])).astype(jnp.bfloat16)
        grad_query = jnp.einsum(
            "qhk,kd->qhd", grad_scores, key_block, preferred_element_type=jnp.float32
        )
        key_gradient = (
            jnp.einsum("qhk,qhd->kd", grad_scores, query_heads, preferred_element_type=jnp.float32)
            * score_scale
        )
        value_gradient = jnp.einsum(
            "qhk,qhd->kd",
            chances.astype(jnp.bfloat16),
            grad_heads,
            preferred_element_type=jnp.float32,
        )
        partials = (grad_query, key_gradient, value_gradient)
        grad_query_sum = grad_query_sum + partials[0]
        key_parts.append(partials[1])
        value_parts.append(partials[2])
    moving = (key_parts[SPAN - 1], value_parts[SPAN - 1])
    for distance in range(SPAN - 2, -1, -1):
        arrived = from_behind((as_sent(moving[0]), as_sent(moving[1])), "ctx", -1)
        moving = (arrived[0] + key_parts[distance], arrived[1] + value_parts[distance])
    kv_width = key_head_array.shape[1]
    wide_keys = lax.dynamic_update_slice_in_dim(
        jnp.zeros((tokens, kv_width), jnp.float32), moving[0], pair_index * HEAD_SIZE, 1
    )
    wide_values = lax.dynamic_update_slice_in_dim(
        jnp.zeros((tokens, kv_width), jnp.float32), moving[1], pair_index * HEAD_SIZE, 1
    )
    grad_keys, grad_values = (
        lax.psum_scatter(
            wide_keys.astype(jnp.bfloat16), "exp", scatter_dimension=0, tiled=True
        ).astype(jnp.float32),
        lax.psum_scatter(
            wide_values.astype(jnp.bfloat16), "exp", scatter_dimension=0, tiled=True
        ).astype(jnp.float32),
    )
    grad_queries = (
        (grad_query_sum * score_scale).astype(jnp.bfloat16).reshape(tokens, head_count * HEAD_SIZE)
    )
    return (
        layer_out,
        grad_resid,
        grad_queries,
        grad_keys.astype(jnp.bfloat16),
        grad_values.astype(jnp.bfloat16),
    )


def solution(mesh):
    placed = (
        P(("ctx", "exp"), None),
        P("ctx", ("head", "exp")),
        P("ctx", "head"),
        P("ctx", "head"),
        P("ctx"),
        P(("head", "exp"), "ctx"),
        P(),
        P(("ctx", "exp"), None),
        P(("ctx", "exp"), None),
        P(("ctx", "exp"), None, "head"),
        P(("ctx", "exp"), None, "head"),
        P(("ctx", "exp"), "head", None),
        P(("ctx", "exp"), None),
    )
    return jax.shard_map(
        local,
        mesh=mesh,
        in_specs=placed,
        out_specs=(
            P(("ctx", "exp"), None),
            P(("ctx", "exp"), None),
            P("ctx", ("head", "exp")),
            P(("ctx", "exp"), "head"),
            P(("ctx", "exp"), "head"),
        ),
        check_vma=False,
    )
```

profile of v0, /device:TPU:0, one launch (start us, length us, event | category | flops | bytes accessed | tf_op | source)
XLA Modules:
  0.0 1220.7 jit_solution(11768855869684749754)
XLA Ops:
  44.9 10.4 collective-permute-start.7
  66.4 177.5 %all-gather.3.cloned.1.call-done = bf16[2048,4096]{1,0:T(8,128)(2,1)} async-done(((bf16[2048,512]{1,0:T(8,128)(2,1)}), bf16[2048,4096]{1,0:T(8,128)(2,1)}) %all-gather.3.cloned.1.call-update) | async-done | bytes 16777232 | tf_op jit(solution)/shard_map/all_gather | solution.py:103
  243.9 9.3 convolution_convert_fusion.1
  255.4 16.5 %reduce-scatter.4.cloned.1.call-done = bf16[64,4096]{1,0:T(8,128)(2,1)} async-done(((bf16[128,4096]{1,0:T(8,128)(2,1)}), bf16[64,4096]{1,0:T(8,128)(2,1)}) %reduce-scatter.4.cloned.1.call-update) | async-done | bytes 524304 | tf_op jit(solution)/shard_map/reduce_scatter | solution.py:105
  272.1 21.1 %all-reduce.4.cloned.1.call-done = bf16[64,4096]{1,0:T(8,128)(2,1)} async-done(((bf16[64,4096]{1,0:T(8,128)(2,1)}), bf16[64,4096]{1,0:T(8,128)(2,1)}) %all-reduce.4.cloned.1.call-update) | async-done | bytes 524304 | tf_op jit(solution)/shard_map/psum | solution.py:111
  296.9 9.7 gather_fusion
  310.0 134.5 %scatter_fusion = bf16[16,48,4096]{2,1,0:T(8,128)(2,1)} fusion(bf16[16,48,4096]{2,1,0:T(8,128)(2,1)} %broadcast.378.clone, s32[512]{0:T(512)S(1)} %bitcast.238, bf16[512,4096]{1,0:T(8,128)(2,1)} %gather_fusion), kind=kCustom, calls=%fused_computation.4 | custom fusion | bytes 12587008 | tf_op jit(solution)/shard_map/scatter | solution.py:131
  444.5 7.4 all-to-all-start
  451.9 9.7 gather_fusion.2
  465.0 134.2 %scatter_fusion.1 = bf16[16,48,4096]{2,1,0:T(8,128)(2,1)} fusion(bf16[16,48,4096]{2,1,0:T(8,128)(2,1)} %broadcast.378.clone.1, s32[512]{0:T(512)S(1)} %bitcast.239, bf16[512,4096]{1,0:T(8,128)(2,1)} %gather_fusion.2), kind=kCustom, calls=%fused_computation.5 | custom fusion | bytes 12587008 | tf_op jit(solution)/shard_map/scatter | solution.py:136
  599.3 14.9 %all-to-all-start.2 = ((bf16[16,48,4096]{2,1,0:T(8,128)(2,1)}), bf16[16,48,4096]{2,1,0:T(8,128)(2,1)}, u32[]{:S(2)}, u32[]{:S(2)}) async-start(bf16[16,48,4096]{2,1,0:T(8,128)(2,1)} %scatter_fusion.1), calls=%async_computation.3 | async-start | bytes 12582912 | tf_op jit(solution)/shard_map/all_to_all | solution.py:147
  633.1 100.7 %all-to-all-done.2 = bf16[16,48,4096]{2,1,0:T(8,128)(2,1)} async-done(((bf16[16,48,4096]{2,1,0:T(8,128)(2,1)}), bf16[16,48,4096]{2,1,0:T(8,128)(2,1)}, u32[]{:S(2)}, u32[]{:S(2)}) %all-to-all-start.2) | async-done | bytes 6291488 | tf_op jit(solution)/shard_map/all_to_all | solution.py:147
  733.8 36.6 %all-to-all-start.1 = ((bf16[16,48,4096]{2,1,0:T(8,128)(2,1)}), bf16[16,48,4096]{2,1,0:T(8,128)(2,1)}, u32[]{:S(2)}, u32[]{:S(2)}) async-start(bf16[16,48,4096]{2,1,0:T(8,128)(2,1)} %bitcast.249), calls=%async_computation.2 | async-start | bytes 12582912 | tf_op jit(solution)/shard_map/all_to_all | solution.py:164
  776.1 6.6 fusion.10
  782.7 8.1 add_convert_fusion
  790.8 99.8 %all-to-all-done.1 = bf16[16,48,4096]{2,1,0:T(8,128)(2,1)} async-done(((bf16[16,48,4096]{2,1,0:T(8,128)(2,1)}), bf16[16,48,4096]{2,1,0:T(8,128)(2,1)}, u32[]{:S(2)}, u32[]{:S(2)}) %all-to-all-start.1) | async-done | bytes 6291488 | tf_op jit(solution)/shard_map/all_to_all | solution.py:164
  890.6 36.7 %all-to-all-start.3 = ((bf16[16,48,4096]{2,1,0:T(8,128)(2,1)}), bf16[16,48,4096]{2,1,0:T(8,128)(2,1)}, u32[]{:S(2)}, u32[]{:S(2)}) async-start(bf16[16,48,4096]{2,1,0:T(8,128)(2,1)} %bitcast.248), calls=%async_computation.4 | async-start | bytes 12582912 | tf_op jit(solution)/shard_map/all_to_all | solution.py:167
  927.5 17.5 %gather_fusion.1 = bf16[512,4096]{1,0:T(8,128)(2,1)} fusion(bf16[16,48,4096]{2,1,0:T(8,128)(2,1)} %all-to-all-done.1, s32[512]{0:T(512)S(1)} %bitcast.236), kind=kCustom, calls=%fused_computation.1 | custom fusion | bytes 8392704 | tf_op jit(solution)/shard_map/gather | solution.py:170
  949.8 97.8 %all-to-all-done.3 = bf16[16,48,4096]{2,1,0:T(8,128)(2,1)} async-done(((bf16[16,48,4096]{2,1,0:T(8,128)(2,1)}), bf16[16,48,4096]{2,1,0:T(8,128)(2,1)}, u32[]{:S(2)}, u32[]{:S(2)}) %all-to-all-start.3) | async-done | bytes 6291488 | tf_op jit(solution)/shard_map/all_to_all | solution.py:167
  1047.6 17.3 %gather_fusion.3 = bf16[512,4096]{1,0:T(8,128)(2,1)} fusion(bf16[16,48,4096]{2,1,0:T(8,128)(2,1)} %all-to-all-done.3, s32[512]{0:T(512)S(1)} %bitcast.237), kind=kCustom, calls=%fused_computation.3 | custom fusion | bytes 8392704 | tf_op jit(solution)/shard_map/gather | solution.py:171
  1069.7 50.9 %all-reduce.6.cloned.1.call-done = (bf16[64,4096]{1,0:T(8,128)(2,1)}, bf16[64,4096]{1,0:T(8,128)(2,1)}) async-done(((bf16[64,4096]{1,0:T(8,128)(2,1)}, bf16[64,4096]{1,0:T(8,128)(2,1)}), (bf16[64,4096]{1,0:T(8,128)(2,1)}, bf16[64,4096]{1,0:T(8,128)(2,1)})) %all-reduce.6.cloned.1.call-update) | async-done | bytes 1048592 | tf_op jit(solution)/shard_map/psum | solution.py:175
  1125.8 22.4 %all-gather.5.cloned.1.call-done = bf16[128,4096]{1,0:T(8,128)(2,1)} async-done(((bf16[64,4096]{1,0:T(8,128)(2,1)}), bf16[128,4096]{1,0:T(8,128)(2,1)}) %all-gather.5.cloned.1.call-update) | async-done | bytes 1048592 | tf_op jit(solution)/shard_map/all_gather | solution.py:182
  1148.1 12.5 %convolution_convert_fusion.2 = bf16[128,2048]{1,0:T(8,128)(2,1)} fusion(bf16[128,4096]{1,0:T(8,128)(2,1)} %all-gather.5.cloned.1.call-done, bf16[2048,4096]{1,0:T(8,128)(2,1)} %all-gather.3.cloned.1.call-done), kind=kOutput, calls=%fused_computation.23 | convolution fusion | flops 2147745792 | bytes 18350080 | tf_op jit(solution)/shard_map/dot_general | solution.py:181
  1200.9 12.7 %reduce-scatter.8.cloned.1.call-done = bf16[64,256]{1,0:T(8,128)(2,1)} async-done(((bf16[128,256]{1,0:T(8,128)(2,1)}), bf16[64,256]{1,0:T(8,128)(2,1)}) %reduce-scatter.8.cloned.1.call-update) | async-done | bytes 32784 | tf_op jit(solution)/shard_map/reduce_scatter | solution.py:237
  (215 shorter events, 140.4 us)
Async XLA Ops:
  7.2 236.7 %all-gather.3.cloned.1.call-start = ((), (), s32[]{:S(2)}) async-start(), calls=%async_computation.7 | async-start | bytes 18874368 | tf_op jit(solution)/shard_map/all_gather | solution.py:103
  7.9 264.0 %reduce-scatter.4.cloned.1.call-start = ((), (), s32[]{:S(2)}) async-start(), calls=%async_computation.8 | async-start | bytes 1572864 | tf_op jit(solution)/shard_map/reduce_scatter | solution.py:105
  8.0 13.6 %collective-permute-start = (s32[128]{0:T(128)}, s32[128]{0:T(128)S(1)}, u32[]{:S(2)}, u32[]{:S(2)}) collective-permute-start(s32[128]{0:T(128)} %param.17), channel_id=1, source_target_pairs={{0,4},{4,8},{8,12},{12,16},{16,20},{20,24},{24,28},{1,5},{5,9},{9,... | collective-permute-start | bytes 1544 | tf_op jit(solution)/shard_map/ppermute | solution.py:21
  13.7 20.3 %collective-permute-start.1 = (bf16[128,128]{1,0:T(8,128)(2,1)S(1)}, bf16[128,128]{1,0:T(8,128)(2,1)S(1)}, u32[]{:S(2)}, u32[]{:S(2)}) collective-permute-start(bf16[128,128]{1,0:T(8,128)(2,1)S(1)} %constant_dynamic-slice_fusion.1), channel_id=1, source_target_pairs={{0,4},{4,8},{8,12},{12,16},{16,20},{20,24},{24,28},{1,5},{5,9},{9,... | collective-permute-start | bytes 98312 | tf_op jit(solution)/shard_map/ppermute | solution.py:21
  18.1 21.7 %collective-permute-start.2 = (bf16[128,128]{0,1:T(8,128)(2,1)S(1)}, bf16[128,128]{0,1:T(8,128)(2,1)S(1)}, u32[]{:S(2)}, u32[]{:S(2)}) collective-permute-start(bf16[128,128]{0,1:T(8,128)(2,1)S(1)} %copy.139), channel_id=1, source_target_pairs={{0,4},{4,8},{8,12},{12,16},{16,20},{20,24},{24,28},{1,5},{5,9},{9,... | collective-permute-start | bytes 98312 | tf_op jit(solution)/shard_map/ppermute | solution.py:21
  34.1 10.8 collective-permute-start.4
  39.8 16.9 %collective-permute-start.5 = (bf16[128,128]{0,1:T(8,128)(2,1)S(1)}, bf16[128,128]{0,1:T(8,128)(2,1)S(1)}, u32[]{:S(2)}, u32[]{:S(2)}) collective-permute-start(bf16[128,128]{0,1:T(8,128)(2,1)S(1)} %collective-permute-done.2), channel_id=1, source_target_pairs={{0,4},{4,8},{8,12},{12,16},{16,20},{20,24},{24,28},{1,5},{5,9},{9,... | collective-permute-start | bytes 98312 | tf_op jit(solution)/shard_map/ppermute | solution.py:21
  44.9 16.9 %collective-permute-start.7 = (bf16[128,128]{1,0:T(8,128)(2,1)S(1)}, bf16[128,128]{1,0:T(8,128)(2,1)S(1)}, u32[]{:S(2)}, u32[]{:S(2)}) collective-permute-start(bf16[128,128]{1,0:T(8,128)(2,1)S(1)} %collective-permute-done.4), channel_id=1, source_target_pairs={{0,4},{4,8},{8,12},{12,16},{16,20},{20,24},{24,28},{1,5},{5,9},{9,... | collective-permute-start | bytes 98312 | tf_op jit(solution)/shard_map/ppermute | solution.py:21
  56.7 8.0 collective-permute-start.8
  253.3 39.9 %all-reduce.4.cloned.1.call-start = ((), (), s32[]{:S(2)}) async-start(), calls=%async_computation.9 | async-start | bytes 1048576 | tf_op jit(solution)/shard_map/psum | solution.py:111
  444.5 154.7 %all-to-all-start = ((bf16[16,48,4096]{2,1,0:T(8,128)(2,1)}), bf16[16,48,4096]{2,1,0:T(8,128)(2,1)}, u32[]{:S(2)}, u32[]{:S(2)}) async-start(bf16[16,48,4096]{2,1,0:T(8,128)(2,1)} %scatter_fusion), calls=%async_computation.1 | async-start | bytes 12582912 | tf_op jit(solution)/shard_map/all_to_all | solution.py:142
  599.3 134.5 %all-to-all-start.2 = ((bf16[16,48,4096]{2,1,0:T(8,128)(2,1)}), bf16[16,48,4096]{2,1,0:T(8,128)(2,1)}, u32[]{:S(2)}, u32[]{:S(2)}) async-start(bf16[16,48,4096]{2,1,0:T(8,128)(2,1)} %scatter_fusion.1), calls=%async_computation.3 | async-start | bytes 12582912 | tf_op jit(solution)/shard_map/all_to_all | solution.py:147
  733.8 156.8 %all-to-all-start.1 = ((bf16[16,48,4096]{2,1,0:T(8,128)(2,1)}), bf16[16,48,4096]{2,1,0:T(8,128)(2,1)}, u32[]{:S(2)}, u32[]{:S(2)}) async-start(bf16[16,48,4096]{2,1,0:T(8,128)(2,1)} %bitcast.249), calls=%async_computation.2 | async-start | bytes 12582912 | tf_op jit(solution)/shard_map/all_to_all | solution.py:164
  890.6 157.0 %all-to-all-start.3 = ((bf16[16,48,4096]{2,1,0:T(8,128)(2,1)}), bf16[16,48,4096]{2,1,0:T(8,128)(2,1)}, u32[]{:S(2)}, u32[]{:S(2)}) async-start(bf16[16,48,4096]{2,1,0:T(8,128)(2,1)} %bitcast.248), calls=%async_computation.4 | async-start | bytes 12582912 | tf_op jit(solution)/shard_map/all_to_all | solution.py:167
  927.3 193.3 %all-reduce.6.cloned.1.call-start = ((), (), s32[]{:S(2)}) async-start(), calls=%async_computation.13 | async-start | bytes 2097152 | tf_op jit(solution)/shard_map/psum | solution.py:175
  1069.7 78.5 %all-gather.5.cloned.1.call-start = ((), (), s32[]{:S(2)}) async-start(), calls=%async_computation.10 | async-start | bytes 1572864 | tf_op jit(solution)/shard_map/all_gather | solution.py:182
  1125.5 75.4 %reduce-scatter.6.cloned.1.call-start = ((), (), s32[]{:S(2)}) async-start(), calls=%async_computation.11 | async-start | bytes 98304 | tf_op jit(solution)/shard_map/reduce_scatter | solution.py:234
  1168.5 5.9 collective-permute-start.9
  1170.0 6.4 collective-permute-start.12
  1174.8 6.3 collective-permute-start.10
  1176.7 6.7 collective-permute-start.13
  1181.1 6.7 collective-permute-start.11
  1183.8 6.7 collective-permute-start.14
  1188.5 25.1 %reduce-scatter.8.cloned.1.call-start = ((), (), s32[]{:S(2)}) async-start(), calls=%async_computation.12 | async-start | bytes 98304 | tf_op jit(solution)/shard_map/reduce_scatter | solution.py:237
  (50 other events, 1304.6 us)
Sparse Core Ops, SparseCore 0:
  10.1 233.8 all-gather.2
  253.4 18.4 reduce-scatter.3
  274.4 18.7 all-reduce.3
  1069.8 50.7 all-reduce.5
  1125.6 22.4 all-gather.4
  1188.6 12.2 reduce-scatter.5
  1203.7 9.8 reduce-scatter.7
where the time goes:
time: 1230 us; the launch traced here: 1220 us
  waiting for transfers between devices  618 us (50%)
  local copies, waits for them, and re-layouts  342 us (28%)
  starting transfers between devices  148 us (12%)
  matrix products  83.3 us (7%)
  between operations  15.5 us (1%)
  other arithmetic  13.8 us (1%)
    all_gather x1, waiting for transfers between devices, local(): out_full = lax.all_gather(out_weight, 'ctx', axis=1, tiled=True)  177 us
    scatter x1, local copies, waits for them, and re-layouts, local(): send_normed = jnp.zeros((expert_count, capacity, model_width), jnp.bfloat...  135 us
    scatter x1, local copies, waits for them, and re-layouts, local(): send_grads = jnp.zeros((expert_count, capacity, model_width), jnp.bfloat1...  134 us
    all_to_all x1, waiting for transfers between devices, local(): lax.all_to_all(send_grads, ('ctx', 'exp'), split_axis=0, concat_axis=0, t...  101 us
    all_to_all x1, waiting for transfers between devices, local(): lax.all_to_all(expert_out.reshape(shape_in), ('ctx', 'exp'), split_axis=0...  99.8 us
    all_to_all x1, waiting for transfers between devices, local(): lax.all_to_all(grad_in.reshape(shape_in), ('ctx', 'exp'), split_axis=0, c...  97.8 us
    ppermute x15, starting transfers between devices, from_behind(): lax.ppermute(value, axis, [(source, source + steps) for source in range(l...  52.1 us
    psum x1, waiting for transfers between devices, local(): lax.psum(moe_share.astype(jnp.bfloat16), 'head').astype(jnp.float32)  50.9 us
  transfers between devices with their start and end apart: 26, of which 18 were waited for; matrix products, arithmetic and copies ran while one was open for 19% of the time, Pallas kernels for 0%

commit v1 on v0

v1 whole, which is shorter than its diff:
```python
import math

import jax
import jax.numpy as jnp
from jax import lax
from jax.experimental import pallas as pl
from jax.experimental.pallas import tpu as pltpu
from jax.sharding import PartitionSpec as P

HEAD_SIZE = 128
QUERY_HEADS = 64
KEY_VALUE_HEADS = 4
SPAN = 4


neg_large = -1e30
eps_norm = 1e-06
bf16 = jnp.bfloat16
f32 = jnp.float32
SCALE = 1.0 / math.sqrt(HEAD_SIZE)
LAST = (((1,), (1,)), ((), ()))
FIRST = (((0,), (0,)), ((), ()))


def dot(a, b, dims=None):
    if dims is None:
        return jnp.dot(a, b, preferred_element_type=f32)
    return lax.dot_general(a, b, dims, preferred_element_type=f32)


def attend_forward(q_ref, k_ref, v_ref, bias_ref, attn_ref, lse_ref):
    keys, values, bias = k_ref[...], v_ref[...], bias_ref[...]
    totals = []
    for head in range(q_ref.shape[1] // HEAD_SIZE):
        part = slice(head * HEAD_SIZE, (head + 1) * HEAD_SIZE)
        scores = dot(q_ref[:, part], keys, LAST) * SCALE + bias
        top = jnp.max(scores, axis=-1, keepdims=True)
        weights = jnp.exp(scores - top)
        total = jnp.sum(weights, axis=-1, keepdims=True)
        attn_ref[:, part] = (dot(weights.astype(bf16), values) / total).astype(bf16)
        totals.append(top + jnp.log(total))
    lse_ref[...] = jnp.concatenate(totals, axis=1)


def attend_backward(
    q_ref, k_ref, v_ref, bias_ref, attn_ref, lse_ref, grad_ref, dq_ref, dk_ref, dv_ref
):
    keys, values, bias = k_ref[...], v_ref[...], bias_ref[...]
    dk_ref[...] = jnp.zeros_like(dk_ref)
    dv_ref[...] = jnp.zeros_like(dv_ref)
    for head in range(q_ref.shape[1] // HEAD_SIZE):
        part = slice(head * HEAD_SIZE, (head + 1) * HEAD_SIZE)
        query, grad = q_ref[:, part], grad_ref[:, part]
        delta = jnp.sum(
            grad.astype(f32) * attn_ref[:, part].astype(f32), axis=-1, keepdims=True
        )
        scores = dot(query, keys, LAST) * SCALE + bias
        probs = jnp.exp(scores - lse_ref[:, head : head + 1])
        dscore = (probs * (dot(grad, values, LAST) - delta)).astype(bf16)
        dq_ref[:, part] = (dot(dscore, keys) * SCALE).astype(bf16)
        dk_ref[...] += dot(dscore, query, FIRST)
        dv_ref[...] += dot(probs.astype(bf16), grad, FIRST)
    dk_ref[...] = dk_ref[...] * SCALE


def run_kernel(body, outs, args, flops):
    moved = sum(a.size * a.dtype.itemsize for a in (*args, *outs))
    return pl.pallas_call(
        body,
        out_shape=outs,
        compiler_params=pltpu.CompilerParams(vmem_limit_bytes=40 * 2**20),
        cost_estimate=pl.CostEstimate(flops=flops, bytes_accessed=moved, transcendentals=0),
    )(*args)


def local(
    residual,
    queries,
    key_head_array,
    value_head_array,
    doc_ids,
    out_weight,
    norm_gain,
    routes,
    gate_probs,
    expert_gate,
    expert_up,
    expert_down,
    grad_out,
):
    C, H, E = lax.axis_size("ctx"), lax.axis_size("head"), lax.axis_size("exp")
    c, h, e = lax.axis_index("ctx"), lax.axis_index("head"), lax.axis_index("exp")
    tokens, features = queries.shape
    head_count = features // HEAD_SIZE
    group_width = QUERY_HEADS // KEY_VALUE_HEADS
    rows, width = residual.shape
    r = rows // H
    cols = width // C
    half = C // 2

    cycle = list(range(0, C, 2)) + list(range(C - 1, 0, -2))
    places = [cycle.index(i) for i in range(C)]
    ahead = [(cycle[i], cycle[(i + 1) % C]) for i in range(C)]
    back = [(d, s) for s, d in ahead]
    place = jnp.asarray(places, jnp.int32)[c]
    cycle_array = jnp.asarray(cycle, jnp.int32)

    def owner(k):
        return cycle_array[lax.rem(place + k + C, C)]

    def to_ahead(x):
        return lax.ppermute(x, "ctx", ahead)

    def to_back(x):
        return lax.ppermute(x, "ctx", back)

    def to_core(x):
        return lax.ppermute(x, "head", [(i, (i + 1) % H) for i in range(H)])

    def exp_from(x, j):
        return lax.ppermute(x, "exp", [((i + j) % E, i) for i in range(E)])

    def exp_to(x, j):
        return lax.ppermute(x, "exp", [(i, (i + j) % E) for i in range(E)])

    def take(x, i, axis=0):
        return lax.dynamic_index_in_dim(x, i, axis, keepdims=False)

    def ring_gather(x):
        found = {0: x}
        f = b = x
        for k in range(1, half):
            f, b = to_ahead(f), to_back(b)
            found[-k], found[k] = f, b
        n = x.shape[0] // 2
        found[half] = jnp.concatenate([to_ahead(f[:n]), to_back(b[n:])], axis=0)
        return found

    def ring_reduce(part):
        far = part(half).astype(bf16)
        n = far.shape[0] // 2
        f, b = to_ahead(far[:n]), to_back(far[n:])
        for k in range(half - 1, 0, -1):
            own_f, own_b = part(k), part(-k)
            if k == half - 1:
                own_f = jnp.concatenate([own_f[:n] + f, own_f[n:]], axis=0)
                own_b = jnp.concatenate([own_b[:n], own_b[n:] + b], axis=0)
            else:
                own_f, own_b = own_f + f, own_b + b
            f, b = to_ahead(own_f.astype(bf16)), to_back(own_b.astype(bf16))
        return part(0) + f + b

    def placed(found, axis=0):
        out = None
        for k, x in found.items():
            x = jnp.expand_dims(x, axis)
            if out is None:
                shape = list(x.shape)
                shape[axis] = C
                out = jnp.zeros(shape, x.dtype)
            out = lax.dynamic_update_slice_in_dim(out, x, owner(k), axis)
        return out

    pair_index = e * head_count // group_width
    own_keys = lax.dynamic_slice_in_dim(key_head_array, pair_index * HEAD_SIZE, HEAD_SIZE, 1)
    own_values = lax.dynamic_slice_in_dim(value_head_array, pair_index * HEAD_SIZE, HEAD_SIZE, 1)
    docs_rows = jnp.broadcast_to(doc_ids.astype(bf16)[None, :], (16, tokens))
    payload = jnp.concatenate([own_keys, own_values, docs_rows], axis=0)
    blocks = [payload] + [
        lax.ppermute(payload, "ctx", [(i, (i + d) % C) for i in range(C)]) for d in range(1, SPAN)
    ]
    keys = jnp.concatenate([b[:tokens] for b in blocks], axis=0)
    values = jnp.concatenate([b[tokens : 2 * tokens] for b in blocks], axis=0)
    key_docs = jnp.concatenate([b[2 * tokens] for b in blocks], axis=0)
    key_pos = jnp.concatenate(
        [(c - d) * tokens + jnp.arange(tokens, dtype=jnp.int32) for d in range(SPAN)]
    )
    query_pos = c * tokens + jnp.arange(tokens, dtype=jnp.int32)
    visible = (
        (doc_ids.astype(bf16)[:, None] == key_docs[None, :])
        & (key_pos[None, :] <= query_pos[:, None])
        & (key_pos[None, :] >= 0)
    )
    bias = jnp.where(visible, 0.0, neg_large).astype(f32)

    gate_mat, up_mat, down_mat = expert_gate[0], expert_up[0], expert_down[0]
    into = jnp.concatenate([gate_mat, to_core(gate_mat), up_mat, to_core(up_mat)], axis=1)
    down = jnp.concatenate([down_mat, to_core(down_mat)], axis=0)
    ff = down.shape[0]

    own_grad_out = take(grad_out.reshape(H, r, width), h)
    grads_own = placed(ring_gather(own_grad_out)).reshape(C * r, width)
    grads = [grads_own] + [exp_from(grads_own, j) for j in range(1, E)]

    expert_count = C * E
    own_routes = take(routes.reshape(H, r, -1), h)
    own_gates = take(gate_probs.reshape(H, r, -1), h)
    chosen = own_routes[:, :, None] == jnp.arange(expert_count, dtype=jnp.int32)
    table = jnp.sum(jnp.where(chosen, own_gates[:, :, None], 0.0), axis=1)
    table = lax.all_gather(table, ("ctx", "exp"), axis=0, tiled=False).reshape(C, E, r, expert_count)
    gates = take(table, c * E + e, 3)
    gates = jnp.roll(jnp.swapaxes(gates, 0, 1), -e, axis=0).reshape(E * C * r, 1)

    own_residual = take(residual.reshape(H, r, C, cols), h)
    residual_cols = lax.all_to_all(jnp.swapaxes(own_residual, 0, 1), "ctx", 0, 0, tiled=True)

    attn, lse = run_kernel(
        attend_forward,
        (
            jax.ShapeDtypeStruct((tokens, features), bf16),
            jax.ShapeDtypeStruct((tokens, head_count), f32),
        ),
        (queries, keys, values, bias),
        4 * tokens * keys.shape[0] * features,
    )

    projected = placed({k: dot(x, out_weight) for k, x in ring_gather(attn).items()})
    projected = projected.reshape(C, E, H, r, cols)
    share = take(projected, h, 2) + to_core(take(projected, 1 - h, 2).astype(bf16))
    attn_proj = take(share, e, 1)
    for j in range(1, E):
        attn_proj = attn_proj + exp_to(take(share, lax.rem(e + j, E), 1).astype(bf16), j)
    hidden = residual_cols.astype(f32) + attn_proj
    gain = lax.dynamic_slice_in_dim(norm_gain, c * cols, cols, 0)
    scaled = (hidden * gain).astype(bf16).reshape(C * r, cols)

    def summed(x):
        return jnp.roll(lax.psum(jnp.roll(x, e, axis=0), ("ctx", "exp")), -e, axis=0)

    squares = jnp.sum(hidden * hidden, axis=-1).reshape(1, C * r)
    squares = summed(jnp.concatenate([squares, jnp.zeros((E - 1, C * r), f32)], axis=0))
    factor = lax.rsqrt(squares / width + eps_norm).reshape(E * C * r, 1)

    found = ring_gather(scaled)
    gathered = [placed(found, 1)]
    near = 1 if half > 2 else 0
    for j in range(1, E):
        if E > 2:
            gathered.append(exp_from(gathered[0], j))
            continue
        first = exp_from(scaled, j)
        others = {k: exp_from(x, j) for k, x in found.items() if abs(k) > near}
        others[0] = first
        if near:
            others[-1], others[1] = to_ahead(first), to_back(first)
        gathered.append(placed(others, 1))
    rows_in = jnp.concatenate(gathered, axis=0).reshape(E * C * r, width)
    rows_grad = jnp.concatenate(grads, axis=0)

    pre = dot(rows_in, into)
    gate_raw, up_raw = pre[:, :ff], pre[:, ff:]
    gate_pre, up_pre = gate_raw * factor, up_raw * factor
    sigma = jax.nn.sigmoid(gate_pre)
    silu_val = gate_pre * sigma
    act = (gates * silu_val * up_pre).astype(bf16)
    back_act = gates * dot(rows_grad, down, LAST)
    slope = sigma * (1.0 + gate_pre * (1.0 - sigma))
    grad_gate = (back_act * up_pre * slope).astype(bf16)
    grad_up = (back_act * silu_val).astype(bf16)
    inner = jnp.sum(grad_gate.astype(f32) * gate_raw + grad_up.astype(f32) * up_raw, axis=-1)
    inner = summed(inner.reshape(E, C * r))[0].reshape(C, r, 1)
    grad_both = jnp.concatenate([grad_gate, grad_up], axis=1)

    def back_part(k):
        weight = lax.dynamic_slice_in_dim(into, owner(k) * cols, cols, 0)
        return dot(grad_both, weight, LAST).reshape(E, C * r, cols)

    back_parts = {k: back_part(k) for k in range(1 - half, half + 1)}
    sums = {k: x[0] for k, x in back_parts.items()}
    for j in range(1, E):
        others = {k: x[j].astype(bf16) for k, x in back_parts.items()}
        if E > 2:
            moved = exp_to(jnp.stack(list(others.values())), j)
            sums = {k: sums[k] + moved[i] for i, k in enumerate(others)}
            continue
        for k in others:
            if abs(k) > near:
                sums[k] = sums[k] + exp_to(others[k], j)
        last = back_parts[0][j]
        if near:
            last = last + to_ahead(others[1]) + to_back(others[-1])
        sums[0] = sums[0] + exp_to(last.astype(bf16), j)
    norm_grad = ring_reduce(lambda k: sums[k]).reshape(C, r, cols)

    own_factor = factor[: C * r].reshape(C, r, 1)
    grad_hidden = (
        take(grads_own.reshape(C, r, C, cols), c, 2).astype(f32)
        + own_factor * gain * norm_grad
        - hidden * (own_factor * own_factor * own_factor * inner / width)
    )
    grad_cols = grad_hidden.astype(bf16)

    outs = dot(act, down).reshape(E, C * r, width)
    out_sum = outs[0]
    for j in range(1, E):
        out_sum = out_sum + exp_to(outs[j].astype(bf16), j)
    out_sum = out_sum.reshape(C, r, width)
    moe_rows = ring_reduce(lambda k: take(out_sum, owner(k)))

    grad_exp = jnp.stack([grad_cols] + [exp_from(grad_cols, j) for j in range(1, E)], axis=1)
    grad_exp = jnp.roll(grad_exp, e, axis=1)
    grad_other = to_core(grad_exp)
    grad_rows = jnp.roll(jnp.stack([grad_exp, grad_other], axis=2), h, axis=2)
    grad_rows = grad_rows.reshape(C, tokens, cols)
    grad_attn = ring_reduce(lambda k: dot(take(grad_rows, owner(k)), out_weight, LAST)).astype(bf16)

    pair = jnp.stack([attn_proj.astype(bf16), grad_cols], axis=1)
    pair = jnp.moveaxis(lax.all_to_all(pair, "ctx", 0, 0, tiled=True), 0, 2).reshape(2, r, width)
    hidden_rows = take(residual.reshape(H, r, width), h).astype(f32) + pair[0].astype(f32)
    layer_rows = (hidden_rows + moe_rows).astype(bf16)

    def both_cores(x):
        return jnp.roll(jnp.stack([x, to_core(x)], axis=0), h, axis=0).reshape(rows, width)

    layer_out, grad_resid = both_cores(layer_rows), both_cores(pair[1])

    span_keys = keys.shape[0]
    grad_queries, key_parts, value_parts = run_kernel(
        attend_backward,
        (
            jax.ShapeDtypeStruct((tokens, features), bf16),
            jax.ShapeDtypeStruct((span_keys, HEAD_SIZE), f32),
            jax.ShapeDtypeStruct((span_keys, HEAD_SIZE), f32),
        ),
        (queries, keys, values, bias, attn, lse, grad_attn),
        10 * tokens * span_keys * features,
    )
    parts = jnp.stack(
        [key_parts.reshape(SPAN, tokens, HEAD_SIZE), value_parts.reshape(SPAN, tokens, HEAD_SIZE)],
        axis=1,
    )
    total = parts[0]
    for d in range(1, SPAN):
        total = total + lax.ppermute(
            parts[d].astype(bf16), "ctx", [(i, (i - d) % C) for i in range(C)]
        )
    total = total.reshape(2, E, rows, HEAD_SIZE)
    groups = jnp.arange(key_head_array.shape[1] // HEAD_SIZE, dtype=jnp.int32)[None, None, :, None]
    pairs = 0.0
    for j in range(E):
        x = take(total, lax.rem(e + j, E), 1)
        if j:
            x = exp_to(x.astype(bf16), j).astype(f32)
        group = lax.rem(e - j + E, E) * head_count // group_width
        pairs = pairs + jnp.where(groups == group, x[:, :, None, :], 0.0)
    pairs = pairs.astype(bf16).reshape(2, rows, key_head_array.shape[1])
    return layer_out, grad_resid, grad_queries, pairs[0], pairs[1]


def solution(mesh):
    placed = (
        P(("ctx", "exp"), None),
        P("ctx", ("head", "exp")),
        P("ctx", "head"),
        P("ctx", "head"),
        P("ctx"),
        P(("head", "exp"), "ctx"),
        P(),
        P(("ctx", "exp"), None),
        P(("ctx", "exp"), None),
        P(("ctx", "exp"), None, "head"),
        P(("ctx", "exp"), None, "head"),
        P(("ctx", "exp"), "head", None),
        P(("ctx", "exp"), None),
    )
    return jax.shard_map(
        local,
        mesh=mesh,
        in_specs=placed,
        out_specs=(
            P(("ctx", "exp"), None),
            P(("ctx", "exp"), None),
            P("ctx", ("head", "exp")),
            P(("ctx", "exp"), "head"),
            P(("ctx", "exp"), "head"),
        ),
        check_vma=False,
    )
```

time: 1230 us -> 585 us (0.48)
  waiting for transfers between devices: 618 us -> 218 us
  local copies, waits for them, and re-layouts: 342 us -> 43.4 us
  blocking collectives: 0 us -> 117 us
  starting transfers between devices: 148 us -> 76.9 us
  matrix products: 83.3 us -> 50.3 us
  other arithmetic: 13.8 us -> 31.8 us
  between operations: 15.5 us -> 28 us
    all_to_all x4 -> x2, waiting for transfers between devices: 298 us -> 0.01 us  [the longest x1 0.01 us: local(): lax.all_to_all(jnp.swapaxes(own_residual, 0, 1), 'ctx', 0, 0, tiled=True)]
    scatter x2 -> x0, local copies, waits for them, and re-layouts: 269 us -> none  [the longest x1 135 us: local(): send_normed = jnp.zeros((expert_count, capacity, model_width), jnp.bfloat...]
    ppermute x15 -> x82, waiting for transfers between devices: 12.4 us -> 218 us  [the longest x26 79.3 us: to_back(): return lax.ppermute(x, 'ctx', back)]
    all_gather x2 -> x0, waiting for transfers between devices: 200 us -> none  [the longest x1 177 us: local(): out_full = lax.all_gather(out_weight, 'ctx', axis=1, tiled=True)]
    all_to_all x4 -> x2, starting transfers between devices: 95.6 us -> 7.9 us  [the longest x1 4.36 us: local(): lax.all_to_all(pair, 'ctx', 0, 0, tiled=True)]
    psum x0 -> x2, blocking collectives: none -> 74.9 us  [summed(): lax.psum(jnp.roll(x, e, axis=0), ('ctx', 'exp'))]
    psum x2 -> x0, waiting for transfers between devices: 71.9 us -> none  [the longest x1 50.9 us: local(): lax.psum(moe_share.astype(jnp.bfloat16), 'head').astype(jnp.float32)]
    gather x4 -> x0, local copies, waits for them, and re-layouts: 54.2 us -> none  [the longest x1 17.5 us: local(): back_out[flat_routes, slots].reshape(row_count, top_count, model_width)]
  transfers between devices with their start and end apart: 26 -> 84, of which waited for: 18 -> 40; matrix products, arithmetic and copies ran while one was open for 19% -> 17% of each run, Pallas kernels for 0% -> 2%
where the time goes in v1:
time: 585 us; the launch traced here: 575 us
  waiting for transfers between devices  218 us (37%)
  blocking collectives  117 us (20%)
  starting transfers between devices  76.9 us (13%)
  matrix products  50.3 us (9%)
  local copies, waits for them, and re-layouts  43.4 us (7%)
  other arithmetic  31.8 us (5%)
  between operations  28 us (5%)
  Pallas kernels  10.3 us (2%)
    ppermute x26, waiting for transfers between devices, to_back(): return lax.ppermute(x, 'ctx', back)  79.3 us
    psum x2, blocking collectives, summed(): lax.psum(jnp.roll(x, e, axis=0), ('ctx', 'exp'))  74.9 us
    ppermute x8, waiting for transfers between devices, exp_from(): return lax.ppermute(x, 'exp', [((i + j) % E, i) for i in range(E)])  50.4 us
    ppermute x26, waiting for transfers between devices, to_ahead(): return lax.ppermute(x, 'ctx', ahead)  44.7 us
    all_gather x1, blocking collectives, local(): lax.all_gather(table, ('ctx', 'exp'), axis=0, tiled=False)  41.8 us
    ppermute x9, waiting for transfers between devices, exp_to(): return lax.ppermute(x, 'exp', [(i, (i + j) % E) for i in range(E)])  39.8 us
    dot_general x17, matrix products, dot(): return lax.dot_general(a, b, dims, preferred_element_type=f32)  31.8 us
    ppermute x26, starting transfers between devices, to_back(): return lax.ppermute(x, 'ctx', back)  21.4 us
  transfers between devices with their start and end apart: 84, of which 40 were waited for; matrix products, arithmetic and copies ran while one was open for 17% of the time, Pallas kernels for 2%

profile of v1, /device:TPU:0, one launch (start us, length us, event | category | flops | bytes accessed | tf_op | source)
XLA Modules:
  0.0 575.0 jit_solution(16729674952422216351)
XLA Ops:
  41.4 41.8 %all-gather.1 = f32[16,32,16]{1,2,0:T(8,128)S(1)} all-gather(f32[1,32,16]{1,2,0:T(8,128)S(1)} %bitcast.378), channel_id=2, replica_groups=mesh['ctx'=8,'head'=2,'exp'=2] {'ctx','exp'}, dimensions={0}, use_global_device_ids=true | all-gather | bytes 34816 | tf_op jit(solution)/shard_map/all_gather | solution.py:200
  100.4 16.6 %collective-permute-done.15 = bf16[32,4096]{1,0:T(8,128)(2,1)S(1)} collective-permute-done((bf16[32,4096]{1,0:T(8,128)(2,1)}, bf16[32,4096]{1,0:T(8,128)(2,1)S(1)}, u32[]{:S(2)}, u32[]{:S(2)}) %collective-permute-start.15) | collective-permute-done | bytes 262176 | tf_op jit(solution)/shard_map/ppermute | solution.py:112
  117.7 7.4 %collective-permute-done.16 = bf16[32,4096]{1,0:T(8,128)(2,1)S(1)} collective-permute-done((bf16[32,4096]{1,0:T(8,128)(2,1)}, bf16[32,4096]{1,0:T(8,128)(2,1)S(1)}, u32[]{:S(2)}, u32[]{:S(2)}) %collective-permute-start.16) | collective-permute-done | bytes 262176 | tf_op jit(solution)/shard_map/ppermute | solution.py:115
  128.3 9.4 %collective-permute-done.4 = bf16[128,2048]{1,0:T(8,128)(2,1)S(1)} collective-permute-done((bf16[128,2048]{1,0:T(8,128)(2,1)S(1)}, bf16[128,2048]{1,0:T(8,128)(2,1)S(1)}, u32[]{:S(2)}, u32[]{:S(2)}) %collective-permute-start.4) | collective-permute-done | bytes 524320 | tf_op jit(solution)/shard_map/ppermute | solution.py:115
  140.3 4.4 collective-permute-done.18
  145.8 5.1 collective-permute-done.5
  152.4 4.4 collective-permute-done.6
  158.1 10.7 %collective-permute-done.8 = bf16[128,2048]{1,0:T(8,128)(2,1)S(1)} collective-permute-done((bf16[128,2048]{1,0:T(8,128)(2,1)S(1)}, bf16[128,2048]{1,0:T(8,128)(2,1)S(1)}, u32[]{:S(2)}, u32[]{:S(2)}) %collective-permute-start.8) | collective-permute-done | bytes 524320 | tf_op jit(solution)/shard_map/ppermute | solution.py:115
  196.2 37.2 %psum.14 = f32[2,256]{1,0:T(2,128)S(1)} all-reduce(f32[2,256]{1,0:T(2,128)S(1)} %fusion.143), channel_id=1, replica_groups=mesh['ctx'=8,'head'=2,'exp'=2] {'ctx','exp'}, use_global_device_ids=true, to_apply=%region_1.3 | all-reduce | flops 512 | bytes 4096 | tf_op jit(solution)/shard_map/psum | solution.py:228
  247.9 6.1 %pad_maximum_fusion = bf16[4096,1536]{1,0:T(8,128)(2,1)S(1)} fusion(bf16[4096,384]{1,0:T(8,128)(2,1)} %collective-permute-done.40, bf16[4096,384]{1,0:T(8,128)(2,1)} %bitcast.351, bf16[4096,384]{1,0:T(8,128)(2,1)} %collective-permute-done.39, bf16[4096,384]{1,0:T(8,128)(2,1)} %bitcast.353), kind=kLoop, calls=%fused_computation | loop fusion | flops 50331648 | bytes 25165824 | tf_op jit(solution)/shard_map/concatenate | solution.py:187
  263.9 29.5 %collective-permute-done.31 = bf16[256,512]{0,1:T(8,128)(2,1)S(1)} collective-permute-done((bf16[256,512]{0,1:T(8,128)(2,1)S(1)}, bf16[256,512]{0,1:T(8,128)(2,1)S(1)}, u32[]{:S(2)}, u32[]{:S(2)}) %collective-permute-start.31) | collective-permute-done | bytes 262176 | tf_op jit(solution)/shard_map/ppermute | solution.py:121
  293.6 5.4 collective-permute-done.32
  319.7 8.4 %fusion.159 = f32[512,1536]{1,0:T(8,128)} fusion(bf16[512,4096]{0,1:T(8,128)(2,1)S(1)} %bitcast.348, bf16[4096,1536]{1,0:T(8,128)(2,1)S(1)} %pad_maximum_fusion), kind=kOutput, calls=%fused_computation.325 | convolution fusion | flops 6442450944 | bytes 19922944 | tf_op jit(solution)/shard_map/dot_general | solution.py:27
  328.1 9.4 %add_reduce_fusion = (f32[512]{0:T(512)S(1)}, bf16[512,768]{1,0:T(8,128)(2,1)}, bf16[512,768]{1,0:T(8,128)(2,1)}) fusion(f32[512,1536]{1,0:T(8,128)} %fusion.159, f32[512]{0:T(512)S(1)} %bitcast.384, f32[512]{0:T(512)S(1)} %mul.187, bf16[384,4096]{1,0:T(8,128)(2,1)} %collective-permute-done.22, bf16[384,4096]{1,0:T(8,128)(2,1)S(1)} %bitcast.387, ...), kind=kOutput, calls=%fused_computation.17 | convolution fusion | flops 3250847232 | bytes 15210496 | tf_op jit(solution)/shard_map/dot_general | solution.py:28
  379.7 37.7 %psum.15 = f32[2,256]{1,0:T(2,128)S(1)} all-reduce(f32[2,256]{1,0:T(2,128)S(1)} %fusion.139), channel_id=1, replica_groups=mesh['ctx'=8,'head'=2,'exp'=2] {'ctx','exp'}, use_global_device_ids=true, to_apply=%region_4.6 | all-reduce | flops 512 | bytes 4096 | tf_op jit(solution)/shard_map/psum | solution.py:228
  420.2 5.5 collective-permute-done.68
  427.1 6.6 %fusion.4 = f32[512,4096]{1,0:T(8,128)S(1)} fusion(bf16[384,4096]{1,0:T(8,128)(2,1)} %collective-permute-done.22, bf16[384,4096]{1,0:T(8,128)(2,1)S(1)} %bitcast.388, f32[512,1536]{1,0:T(8,128)} %fusion.159, f32[512]{0:T(512)S(1)} %bitcast.385, f32[512]{0:T(512)S(1)} %mul.187), kind=kOutput, calls=%fused_computation.9 | convolution fusion | flops 3237347328 | bytes 17829888 | tf_op jit(solution)/shard_map/dot_general | solution.py:27
  441.4 4.4 all-to-all-start.1
  454.5 32.5 %collective-permute-done.57 = bf16[256,4096]{1,0:T(8,128)(2,1)} collective-permute-done((bf16[256,4096]{1,0:T(8,128)(2,1)}, bf16[256,4096]{1,0:T(8,128)(2,1)}, u32[]{:S(2)}, u32[]{:S(2)}) %collective-permute-start.57) | collective-permute-done | bytes 2097184 | tf_op jit(solution)/shard_map/ppermute | solution.py:124
  509.6 8.6 %collective-permute-done.71 = bf16[128,2048]{1,0:T(8,128)(2,1)} collective-permute-done((bf16[128,2048]{1,0:T(8,128)(2,1)}, bf16[128,2048]{1,0:T(8,128)(2,1)}, u32[]{:S(2)}, u32[]{:S(2)}) %collective-permute-start.71) | collective-permute-done | bytes 524320 | tf_op jit(solution)/shard_map/ppermute | solution.py:112
  528.9 5.1 collective-permute-done.64
  537.0 8.2 %collective-permute-done.76 = bf16[128,2048]{1,0:T(8,128)(2,1)S(1)} collective-permute-done((bf16[128,2048]{1,0:T(8,128)(2,1)S(1)}, bf16[128,2048]{1,0:T(8,128)(2,1)S(1)}, u32[]{:S(2)}, u32[]{:S(2)}) %collective-permute-start.76) | collective-permute-done | bytes 524320 | tf_op jit(solution)/shard_map/ppermute | solution.py:115
  549.9 5.7 collective-permute-done.77
  555.8 6.0 %shard_map.183 = (bf16[128,2048]{1,0:T(8,128)(2,1)}, f32[512,128]{1,0:T(8,128)S(1)}, f32[512,128]{1,0:T(8,128)S(1)}) custom-call(bf16[128,2048]{1,0:T(8,128)(2,1)S(1)} %copy-done.2, bf16[512,128]{1,0:T(8,128)(2,1)S(1)} %pad_maximum_fusion.14.k_ref, bf16[512,128]{1,0:T(8,128)(2,1)S(1)} %pad_maximum_fusion.15.v_ref, f32[128,512]{1,0:T(8,128)S(1)} %and_select_fusion.bias_ref, ...), custom_call_target="tpu_custom_call" | custom-call | flops 1342177280 | bytes 3153920 | tf_op jit(solution)/shard_map/pallas_call | solution.py:68
  (401 shorter events, 230.9 us)
Async XLA Ops:
  13.5 83.5 %collective-permute-start.13 = (bf16[32,4096]{1,0:T(8,128)(2,1)}, bf16[32,4096]{1,0:T(8,128)(2,1)}, u32[]{:S(2)}, u32[]{:S(2)}) collective-permute-start(bf16[32,4096]{1,0:T(8,128)(2,1)} %get-tuple-element.36), channel_id=1, source_target_pairs={{0,8},{8,16},{16,24},{24,28},{28,20},{20,12},{12,4},{4,0},{1,9},{9... | collective-permute-start | bytes 786440 | tf_op jit(solution)/shard_map/ppermute | solution.py:112
  16.5 82.2 %collective-permute-start.14 = (bf16[32,4096]{1,0:T(8,128)(2,1)}, bf16[32,4096]{1,0:T(8,128)(2,1)}, u32[]{:S(2)}, u32[]{:S(2)}) collective-permute-start(bf16[32,4096]{1,0:T(8,128)(2,1)} %get-tuple-element.36), channel_id=1, source_target_pairs={{8,0},{16,8},{24,16},{28,24},{20,28},{12,20},{4,12},{0,4},{9,1},{1... | collective-permute-start | bytes 786440 | tf_op jit(solution)/shard_map/ppermute | solution.py:115
  16.6 71.8 %collective-permute-start = (bf16[272,128]{1,0:T(8,128)(2,1)S(1)}, bf16[272,128]{1,0:T(8,128)(2,1)S(1)}, u32[]{:S(2)}, u32[]{:S(2)}) collective-permute-start(bf16[272,128]{1,0:T(8,128)(2,1)S(1)} %pad_maximum_fusion.16), channel_id=1, source_target_pairs={{0,4},{4,8},{8,12},{12,16},{16,20},{20,24},{24,28},{28,0},{1,5},{5... | collective-permute-start | bytes 208904 | tf_op jit(solution)/shard_map/ppermute | solution.py:170
  18.6 70.0 %collective-permute-start.1 = (bf16[272,128]{1,0:T(8,128)(2,1)S(1)}, bf16[272,128]{1,0:T(8,128)(2,1)S(1)}, u32[]{:S(2)}, u32[]{:S(2)}) collective-permute-start(bf16[272,128]{1,0:T(8,128)(2,1)S(1)} %pad_maximum_fusion.16), channel_id=1, source_target_pairs={{0,8},{4,12},{8,16},{12,20},{16,24},{20,28},{24,0},{28,4},{1,9},{5... | collective-permute-start | bytes 208904 | tf_op jit(solution)/shard_map/ppermute | solution.py:170
  20.2 68.9 %collective-permute-start.2 = (bf16[272,128]{1,0:T(8,128)(2,1)S(1)}, bf16[272,128]{1,0:T(8,128)(2,1)}, u32[]{:S(2)}, u32[]{:S(2)}) collective-permute-start(bf16[272,128]{1,0:T(8,128)(2,1)S(1)} %pad_maximum_fusion.16), channel_id=1, source_target_pairs={{0,12},{4,16},{8,20},{12,24},{16,28},{20,0},{24,4},{28,8},{1,13},{... | collective-permute-start | bytes 208904 | tf_op jit(solution)/shard_map/ppermute | solution.py:170
  23.7 164.9 %all-to-all-start = ((bf16[8,32,512]{2,1,0:T(8,128)(2,1)}), bf16[8,32,512]{2,1,0:T(8,128)(2,1)S(1)}, u32[]{:S(2)}, u32[]{:S(2)}) async-start(bf16[8,32,512]{2,1,0:T(8,128)(2,1)} %bitcast.321), calls=%async_computation | async-start | bytes 524288 | tf_op jit(solution)/shard_map/all_to_all | solution.py:205
  88.5 157.4 %collective-permute-start.39 = (bf16[4096,384]{1,0:T(8,128)(2,1)}, bf16[4096,384]{1,0:T(8,128)(2,1)}, u32[]{:S(2)}, u32[]{:S(2)}) collective-permute-start(bf16[4096,384]{1,0:T(8,128)(2,1)} %bitcast.352), channel_id=1, source_target_pairs={{0,2},{2,0},{1,3},{3,1},{4,6},{6,4},{5,7},{7,5},{8,10},{10,8},{9,1... | collective-permute-start | bytes 9437192 | tf_op jit(solution)/shard_map/ppermute | solution.py:118
  88.6 159.3 %collective-permute-start.40 = (bf16[4096,384]{1,0:T(8,128)(2,1)}, bf16[4096,384]{1,0:T(8,128)(2,1)}, u32[]{:S(2)}, u32[]{:S(2)}) collective-permute-start(bf16[4096,384]{1,0:T(8,128)(2,1)} %bitcast.350), channel_id=1, source_target_pairs={{0,2},{2,0},{1,3},{3,1},{4,6},{6,4},{5,7},{7,5},{8,10},{10,8},{9,1... | collective-permute-start | bytes 9437192 | tf_op jit(solution)/shard_map/ppermute | solution.py:118
  89.1 238.9 %collective-permute-start.22 = (bf16[384,4096]{1,0:T(8,128)(2,1)}, bf16[384,4096]{1,0:T(8,128)(2,1)}, u32[]{:S(2)}, u32[]{:S(2)}) collective-permute-start(bf16[384,4096]{1,0:T(8,128)(2,1)} %bitcast.386), channel_id=1, source_target_pairs={{0,2},{2,0},{1,3},{3,1},{4,6},{6,4},{5,7},{7,5},{8,10},{10,8},{9,1... | collective-permute-start | bytes 9437192 | tf_op jit(solution)/shard_map/ppermute | solution.py:118
  97.0 29.1 %collective-permute-start.3 = (bf16[128,2048]{1,0:T(8,128)(2,1)S(1)}, bf16[128,2048]{1,0:T(8,128)(2,1)S(1)}, u32[]{:S(2)}, u32[]{:S(2)}) collective-permute-start(bf16[128,2048]{1,0:T(8,128)(2,1)S(1)} %get-tuple-element.12.attn_ref), channel_id=1, source_target_pairs={{0,8},{8,16},{16,24},{24,28},{28,20},{20,12},{12,4},{4,0},{1,9},{9... | collective-permute-start | bytes 1572872 | tf_op jit(solution)/shard_map/ppermute | solution.py:112
  192.4 44.2 %collective-permute-start.23 = (bf16[256,512]{0,1:T(8,128)(2,1)}, bf16[256,512]{0,1:T(8,128)(2,1)}, u32[]{:S(2)}, u32[]{:S(2)}) collective-permute-start(bf16[256,512]{0,1:T(8,128)(2,1)} %copy.76), channel_id=1, source_target_pairs={{0,8},{8,16},{16,24},{24,28},{28,20},{20,12},{12,4},{4,0},{1,9},{9... | collective-permute-start | bytes 786440 | tf_op jit(solution)/shard_map/ppermute | solution.py:112
  193.7 46.3 %collective-permute-start.24 = (bf16[256,512]{0,1:T(8,128)(2,1)}, bf16[256,512]{0,1:T(8,128)(2,1)}, u32[]{:S(2)}, u32[]{:S(2)}) collective-permute-start(bf16[256,512]{0,1:T(8,128)(2,1)} %copy.76), channel_id=1, source_target_pairs={{8,0},{16,8},{24,16},{28,24},{20,28},{12,20},{4,12},{0,4},{9,1},{1... | collective-permute-start | bytes 786440 | tf_op jit(solution)/shard_map/ppermute | solution.py:115
  240.0 88.1 %collective-permute-start.21 = (bf16[256,4096]{1,0:T(8,128)(2,1)}, bf16[256,4096]{1,0:T(8,128)(2,1)}, u32[]{:S(2)}, u32[]{:S(2)}) collective-permute-start(bf16[256,4096]{1,0:T(8,128)(2,1)} %bitcast.53), channel_id=1, source_target_pairs={{1,0},{0,1},{3,2},{2,3},{5,4},{4,5},{7,6},{6,7},{9,8},{8,9},{11,10... | collective-permute-start | bytes 6291464 | tf_op jit(solution)/shard_map/ppermute | solution.py:121
  247.9 66.3 %collective-permute-start.37 = (bf16[256,512]{0,1:T(8,128)(2,1)S(1)}, bf16[256,512]{0,1:T(8,128)(2,1)S(1)}, u32[]{:S(2)}, u32[]{:S(2)}) collective-permute-start(bf16[256,512]{0,1:T(8,128)(2,1)S(1)} %collective-permute-done.36), channel_id=1, source_target_pairs={{0,8},{8,16},{16,24},{24,28},{28,20},{20,12},{12,4},{4,0},{1,9},{9... | collective-permute-start | bytes 786440 | tf_op jit(solution)/shard_map/ppermute | solution.py:112
  260.4 33.0 %collective-permute-start.31 = (bf16[256,512]{0,1:T(8,128)(2,1)S(1)}, bf16[256,512]{0,1:T(8,128)(2,1)S(1)}, u32[]{:S(2)}, u32[]{:S(2)}) collective-permute-start(bf16[256,512]{0,1:T(8,128)(2,1)S(1)} %collective-permute-done.25), channel_id=1, source_target_pairs={{1,0},{0,1},{3,2},{2,3},{5,4},{4,5},{7,6},{6,7},{9,8},{8,9},{11,10... | collective-permute-start | bytes 786440 | tf_op jit(solution)/shard_map/ppermute | solution.py:121
  262.9 36.2 %collective-permute-start.32 = (bf16[256,512]{0,1:T(8,128)(2,1)S(1)}, bf16[256,512]{0,1:T(8,128)(2,1)S(1)}, u32[]{:S(2)}, u32[]{:S(2)}) collective-permute-start(bf16[256,512]{0,1:T(8,128)(2,1)S(1)} %collective-permute-done.26), channel_id=1, source_target_pairs={{1,0},{0,1},{3,2},{2,3},{5,4},{4,5},{7,6},{6,7},{9,8},{8,9},{11,10... | collective-permute-start | bytes 786440 | tf_op jit(solution)/shard_map/ppermute | solution.py:121
  340.6 31.8 %collective-permute-start.41 = (bf16[256,512]{1,0:T(8,128)(2,1)S(1)}, bf16[256,512]{1,0:T(8,128)(2,1)S(1)}, u32[]{:S(2)}, u32[]{:S(2)}) collective-permute-start(bf16[256,512]{1,0:T(8,128)(2,1)S(1)} %slice.487), channel_id=1, source_target_pairs={{0,8},{8,16},{16,24},{24,28},{28,20},{20,12},{12,4},{4,0},{1,9},{9... | collective-permute-start | bytes 786440 | tf_op jit(solution)/shard_map/ppermute | solution.py:112
  374.7 42.8 %collective-permute-start.43 = (bf16[256,512]{1,0:T(8,128)(2,1)}, bf16[256,512]{1,0:T(8,128)(2,1)}, u32[]{:S(2)}, u32[]{:S(2)}) collective-permute-start(bf16[256,512]{1,0:T(8,128)(2,1)} %fusion.56), channel_id=1, source_target_pairs={{0,1},{1,0},{2,3},{3,2},{4,5},{5,4},{6,7},{7,6},{8,9},{9,8},{10,11... | collective-permute-start | bytes 786440 | tf_op jit(solution)/shard_map/ppermute | solution.py:124
  376.3 41.2 %collective-permute-start.50 = (bf16[256,512]{1,0:T(8,128)(2,1)}, bf16[256,512]{1,0:T(8,128)(2,1)}, u32[]{:S(2)}, u32[]{:S(2)}) collective-permute-start(bf16[256,512]{1,0:T(8,128)(2,1)} %fusion.54), channel_id=1, source_target_pairs={{0,8},{8,16},{16,24},{24,28},{28,20},{20,12},{12,4},{4,0},{1,9},{9... | collective-permute-start | bytes 786440 | tf_op jit(solution)/shard_map/ppermute | solution.py:112
  378.3 39.2 %collective-permute-start.56 = (bf16[256,512]{1,0:T(8,128)(2,1)}, bf16[256,512]{1,0:T(8,128)(2,1)}, u32[]{:S(2)}, u32[]{:S(2)}) collective-permute-start(bf16[256,512]{1,0:T(8,128)(2,1)} %fusion.50), channel_id=1, source_target_pairs={{8,0},{16,8},{24,16},{28,24},{20,28},{12,20},{4,12},{0,4},{9,1},{1... | collective-permute-start | bytes 786440 | tf_op jit(solution)/shard_map/ppermute | solution.py:115
  438.7 48.4 %collective-permute-start.57 = (bf16[256,4096]{1,0:T(8,128)(2,1)}, bf16[256,4096]{1,0:T(8,128)(2,1)}, u32[]{:S(2)}, u32[]{:S(2)}) collective-permute-start(bf16[256,4096]{1,0:T(8,128)(2,1)} %slice.478), channel_id=1, source_target_pairs={{0,1},{1,0},{2,3},{3,2},{4,5},{5,4},{6,7},{7,6},{8,9},{9,8},{10,11... | collective-permute-start | bytes 6291464 | tf_op jit(solution)/shard_map/ppermute | solution.py:124
  441.4 60.0 %all-to-all-start.1 = ((bf16[8,2,32,512]{3,2,1,0:T(8,128)(2,1)}), bf16[8,2,32,512]{3,2,1,0:T(8,128)(2,1)}, u32[]{:S(2)}, u32[]{:S(2)}) async-start(bf16[8,2,32,512]{3,2,1,0:T(8,128)(2,1)} %copy.79), calls=%async_computation.1 | async-start | bytes 1048576 | tf_op jit(solution)/shard_map/all_to_all | solution.py:308
  448.9 48.7 %collective-permute-start.70 = (bf16[64,2048]{1,0:T(8,128)(2,1)S(1)}, bf16[64,2048]{1,0:T(8,128)(2,1)S(1)}, u32[]{:S(2)}, u32[]{:S(2)}) collective-permute-start(bf16[64,2048]{1,0:T(8,128)(2,1)S(1)} %get-tuple-element.31), channel_id=1, source_target_pairs={{0,8},{8,16},{16,24},{24,28},{28,20},{20,12},{12,4},{4,0},{1,9},{9... | collective-permute-start | bytes 786440 | tf_op jit(solution)/shard_map/ppermute | solution.py:112
  451.7 47.0 %collective-permute-start.74 = (bf16[64,2048]{1,0:T(8,128)(2,1)S(1)}, bf16[64,2048]{1,0:T(8,128)(2,1)S(1)}, u32[]{:S(2)}, u32[]{:S(2)}) collective-permute-start(bf16[64,2048]{1,0:T(8,128)(2,1)S(1)} %get-tuple-element.32), channel_id=1, source_target_pairs={{8,0},{16,8},{24,16},{28,24},{20,28},{12,20},{4,12},{0,4},{9,1},{1... | collective-permute-start | bytes 786440 | tf_op jit(solution)/shard_map/ppermute | solution.py:115
  (93 other events, 1173.6 us)
